TPU v7x, 256 devices: a whole 4x4x8 slice. The times are simulated.
256 devices in a mesh: chan: 32 (over y, x, core), band: 8 (over z).
Axes of the slice: x: 4, y: 4, z: 8, core: 2. Of those that a mesh axis runs over, the one named last changes fastest.
Arguments:
- spectra: bfloat16 [2, 30, 512, 8192], P(None, None, 'chan', 'band'), may hold values from -6 to 6
- source_block: int32 [1], replicated, may hold values from 0 to 127
- segment_flags: int32 [30], replicated, may hold values from 0 to 1, as said below
Outputs:
- correlations: float32 [64, 8, 1024, 1024], P(None, 'band', 'chan')
Inputs may be any that keep to these rules, and one draw needn't show every extreme that they name: `segment_flags`: at least one segment is valid.
All inputs are finite; a program needn't handle non-finite values.
Results may differ from a plain program's by a relative error of at most 0.0037.
Values may be sent and summed in bfloat16 or wider, within the bound.
A program may use at most 128 MiB of HBM per device.

v0:
```python
import math
import jax
import jax.numpy as jnp
from jax import lax
from jax.sharding import PartitionSpec as P

LAGS = 1024
F = 512
SRC = 64
RB = 1024


def spread(block, axis, owner):
    block = jnp.where(lax.axis_index(axis) == owner, block, jnp.zeros_like(block))
    return lax.psum(block, axis)


def lag_table():
    frequency = jnp.arange(F, dtype=jnp.int32)[:, None]
    shifted_lag = jnp.arange(LAGS, dtype=jnp.int32)[None, :] - LAGS // 2
    phase_index = frequency * shifted_lag % LAGS
    phase_angle = 2.0 * math.pi / LAGS * phase_index.astype(jnp.float32)
    weight = jnp.where(frequency == 0, 1.0, 2.0).astype(jnp.float32) / jnp.sqrt(jnp.float32(2 * F))
    cosine_component = weight * jnp.cos(phase_angle)
    sin_part = -weight * jnp.sin(phase_angle)
    return jnp.stack([cosine_component, sin_part], axis=1).astype(jnp.bfloat16)


def stack_segment_windows(source, receiver_traces, valid_mask, valid_window_count):
    masked = source * valid_mask[None, :, None, None]
    left_real = jnp.concatenate([masked[0], masked[1]], axis=0)
    left_imaginary = jnp.concatenate([masked[1], -masked[0]], axis=0)
    left_operand = jnp.concatenate([left_real, left_imaginary], axis=2)
    bins = receiver_traces.shape[2]
    width = receiver_traces.shape[3]
    right_side = receiver_traces.reshape(2 * receiver_traces.shape[1], bins, width)
    summed = lax.dot_general(
        left_operand, right_side, (((0,), (0,)), ((1,), (1,))), preferred_element_type=jnp.float32
    )
    cross_spectrum_product = (summed / valid_window_count).astype(jnp.bfloat16)
    return cross_spectrum_product.reshape(bins, 2, SRC, width)


def local(spectra, source_block, segment_flags):
    first_channel = source_block[0] * SRC
    owner_band = first_channel // RB
    offset = first_channel - owner_band * RB
    local_source = lax.dynamic_slice_in_dim(spectra, offset, SRC, 3)
    source = spread(local_source, "band", owner_band)
    valid_mask = segment_flags.astype(jnp.bfloat16)
    valid_window_count = jnp.sum(segment_flags).astype(jnp.float32)
    lag_weights = lag_table()
    cross_spectrum_product = stack_segment_windows(source, spectra, valid_mask, valid_window_count)
    lagged_correlation = lax.dot_general(
        lax.all_to_all(cross_spectrum_product, "chan", split_axis=3, concat_axis=0, tiled=True),
        lag_weights,
        (((0, 1), (0, 1)), ((), ())),
        preferred_element_type=jnp.float32,
    )
    return lagged_correlation[:, None]


def solution(mesh):
    return jax.shard_map(
        local,
        mesh=mesh,
        in_specs=(P(None, None, "chan", "band"), P(), P()),
        out_specs=P(None, "band", "chan", None),
        check_vma=False,
    )
```

profile of v0, /device:TPU:32, one launch (start us, length us, event | category | flops | bytes accessed | tf_op | source)
XLA Modules:
  0.0 248.0 jit_solution(11593618754978882445)
XLA Ops:
  6.5 0.0 copy-start
  6.5 0.0 all-reduce.2.cloned.1.call-start
  7.4 0.7 copy-done
  8.1 0.1 constant_dynamic-slice_fusion
  8.2 0.8 copy_select_fusion
  9.0 0.0 all-reduce.2.cloned.1.call-update
  9.0 1.4 fusion.20
  11.0 73.7 %all-reduce.2.cloned.1.call-done = bf16[2,30,16,64]{3,1,2,0:T(8,128)(2,1)} async-done(((bf16[2,30,16,64]{3,1,2,0:T(8,128)(2,1)}), bf16[2,30,16,64]{3,1,2,0:T(8,128)(2,1)}) %all-reduce.2.cloned.1.call-update) | async-done | bytes 122896 | tf_op jit(solution)/shard_map/psum | solution.py:15
  84.7 1.0 broadcast_multiply_fusion
  85.8 5.1 %divide_convert_fusion = bf16[16,128,1024]{2,1,0:T(8,128)(2,1)} fusion(f32[]{:T(128)S(6)} %convert_element_type.27, bf16[60,16,1024]{2,1,0:T(8,128)(2,1)S(1)} %bitcast.25, bf16[30,16,64]{2,0,1:T(8,128)(2,1)S(1)} %fusion.19, bf16[30,16,64]{2,0,1:T(8,128)(2,1)S(1)} %get-tuple-element.6, bf16[30,16,64]{2,0,1:T(8,128)(2,1)S(1)} %get-tuple-element.5), kind=kOutput, calls=%fused_computation | convolution fusion | flops 256835584 | bytes 6344708 | tf_op jit(solution)/shard_map/dot_general | solution.py:37
  90.9 20.3 %copy.16 = bf16[16,2,64,1024]{2,1,0,3:T(2,128)(2,1)} copy(bf16[16,2,64,1024]{3,2,1,0:T(8,128)(2,1)} %bitcast.30) | data formatting | bytes 8388608 | tf_op jit(solution)/shard_map/reshape | solution.py:41
  111.2 13.9 %reshape.165 = bf16[32,2,32768]{2,1,0:T(2,128)(2,1)} reshape(bf16[1024,16,2,64]{3,2,1,0:T(2,128)(2,1)} %bitcast.26) | data formatting | bytes 8388608
  125.1 7.4 %all-to-all-start = ((bf16[32,2,32768]{2,1,0:T(2,128)(2,1)}), bf16[32,2,32768]{2,1,0:T(2,128)(2,1)}, u32[]{:S(2)}, u32[]{:S(2)}) async-start(bf16[32,2,32768]{2,1,0:T(2,128)(2,1)} %reshape.165), calls=%async_computation | async-start | bytes 8388608 | tf_op jit(solution)/shard_map/all_to_all | solution.py:55
  132.5 9.4 %multiply_convert_fusion.1 = (bf16[512,1,1024]{2,0,1:T(8,128)(2,1)S(1)}, bf16[512,1,1024]{2,0,1:T(8,128)(2,1)}) fusion(s32[1024]{0:T(1024)S(1)} %iota_add_fusion, f32[512]{0:T(512)S(1)} %get-tuple-element.11, f32[512]{0:T(512)S(1)} %get-tuple-element.12), kind=kLoop, calls=%fused_computation.13 | loop fusion | flops 9437184 | bytes 2105344 | tf_op jit(solution)/shard_map/convert
  141.9 43.9 %all-to-all-done = bf16[32,2,32768]{2,1,0:T(2,128)(2,1)} async-done(((bf16[32,2,32768]{2,1,0:T(2,128)(2,1)}), bf16[32,2,32768]{2,1,0:T(2,128)(2,1)}, u32[]{:S(2)}, u32[]{:S(2)}) %all-to-all-start) | async-done | bytes 4194336 | tf_op jit(solution)/shard_map/all_to_all | solution.py:55
  185.8 13.6 %reshape.166 = bf16[1024,16,2,64]{3,2,1,0:T(2,128)(2,1)} reshape(bf16[32,2,32768]{2,1,0:T(2,128)(2,1)} %all-to-all-done) | data formatting | bytes 8388608
  199.4 9.8 %copy.17 = bf16[16,2,64,1024]{2,3,1,0:T(8,128)(2,1)} copy(bf16[16,2,64,1024]{2,1,0,3:T(2,128)(2,1)} %bitcast.27) | data formatting | bytes 8388608 | tf_op jit(solution)/shard_map/all_to_all | solution.py:55
  209.2 9.5 %copy.18 = bf16[32,16,2,64,32]{3,4,2,1,0:T(8,128)(2,1)} copy(bf16[32,16,2,64,32]{3,4,0,2,1:T(8,128)(2,1)} %bitcast.28) | data formatting | bytes 8388608 | tf_op jit(solution)/shard_map/all_to_all | solution.py:55
  218.7 12.0 %copy.19 = bf16[512,2,64,32]{0,3,1,2:T(8,128)(2,1)} copy(bf16[512,2,64,32]{2,3,1,0:T(8,128)(2,1)} %bitcast.29) | data formatting | bytes 8388608 | tf_op jit(solution)/shard_map/all_to_all | solution.py:55
  230.7 10.4 %convolution_bitcast_fusion = f32[64,1,32,1024]{3,2,1,0:T(8,128)} fusion(bf16[512,2,64,32]{0,3,1,2:T(8,128)(2,1)} %copy.19, bf16[512,1,1024]{2,0,1:T(8,128)(2,1)} %get-tuple-element.8, bf16[512,1,1024]{2,0,1:T(8,128)(2,1)S(1)} %get-tuple-element.7), kind=kOutput, calls=%fused_computation.1 | convolution fusion | flops 4296015872 | bytes 14680064 | tf_op jit(solution)/shard_map/dot_general | solution.py:54
  (4 shorter events, 0.0 us)
Async XLA Ops:
  6.5 1.6 copy-start
  6.5 78.1 %all-reduce.2.cloned.1.call-start = ((), (), s32[]{:S(2)}) async-start(), calls=%async_computation.1 | async-start | bytes 524288 | tf_op jit(solution)/shard_map/psum | solution.py:15
  125.1 60.7 %all-to-all-start = ((bf16[32,2,32768]{2,1,0:T(2,128)(2,1)}), bf16[32,2,32768]{2,1,0:T(2,128)(2,1)}, u32[]{:S(2)}, u32[]{:S(2)}) async-start(bf16[32,2,32768]{2,1,0:T(2,128)(2,1)} %reshape.165), calls=%async_computation | async-start | bytes 8388608 | tf_op jit(solution)/shard_map/all_to_all | solution.py:55
Sparse Core Ops, SparseCore 0:
  9.7 74.9 all-reduce.1
where the time goes:
time: 250 us; the launch traced here: 248 us
  waiting for transfers between devices  118 us (47%)
  local copies, waits for them, and re-layouts  80 us (32%)
  matrix products  15.5 us (6%)
  between operations  14.8 us (6%)
  other arithmetic  12.5 us (5%)
  starting transfers between devices  7.4 us (3%)
    psum x1, waiting for transfers between devices, spread(): return lax.psum(block, axis)  73.7 us
    all_to_all x1, waiting for transfers between devices, local(): lax.all_to_all(cross_spectrum_product, 'chan', split_axis=3, concat_axis=...  43.9 us
    all_to_all x3, local copies, waits for them, and re-layouts, local(): lax.all_to_all(cross_spectrum_product, 'chan', split_axis=3, concat_axis=...  31.3 us
    unnamed x4, local copies, waits for them, and re-layouts  28.3 us
    reshape x1, local copies, waits for them, and re-layouts, stack_segment_windows(): return cross_spectrum_product.reshape(bins, 2, SRC, width)  20.3 us
    dot_general x1, matrix products, local(): lax.dot_general(lax.all_to_all(cross_spectrum_product, 'chan', split_axis...  10.4 us
    another operation x1, other arithmetic  9.35 us
    all_to_all x1, starting transfers between devices, local(): lax.all_to_all(cross_spectrum_product, 'chan', split_axis=3, concat_axis=...  7.4 us
  transfers between devices with their start and end apart: 2, of which 2 were waited for; matrix products, arithmetic and copies ran while one was open for 4% of the time, Pallas kernels for 0%

commit v1 on v0

--- a/solution.py
+++ b/solution.py
@@ -10,9 +10,13 @@
 RB = 1024
 
 
+def feed_cycles_by_axis(inp, chip_axis):
+    return jnp.sum(jax.lax.all_gather(inp, chip_axis), axis=0)
+
+
 def spread(block, axis, owner):
     block = jnp.where(lax.axis_index(axis) == owner, block, jnp.zeros_like(block))
-    return lax.psum(block, axis)
+    return feed_cycles_by_axis(block, axis)
 
 
 def lag_table():

time: 250 us -> 193 us (0.77)
  waiting for transfers between devices: 118 us -> 44.6 us
  blocking collectives: 0 us -> 31.9 us
  between operations: 14.8 us -> 1.41 us
    psum x1 -> x0, waiting for transfers between devices: 73.7 us -> none  [spread(): return lax.psum(block, axis)]
    all_gather x0 -> x1, blocking collectives: none -> 31.9 us  [feed_cycles_by_axis(): return jnp.sum(jax.lax.all_gather(inp, chip_axis), axis=0)]
  transfers between devices with their start and end apart: 2 -> 1, of which waited for: 2 -> 1; matrix products, arithmetic and copies ran while one was open for 4% -> 5% of each run, Pallas kernels for 0% -> 0%
where the time goes in v1:
time: 193 us; the launch traced here: 191 us
  local copies, waits for them, and re-layouts  79.2 us (41%)
  waiting for transfers between devices  44.6 us (23%)
  blocking collectives  31.9 us (17%)
  matrix products  15.6 us (8%)
  other arithmetic  11 us (6%)
  starting transfers between devices  7.63 us (4%)
    all_to_all x1, waiting for transfers between devices, local(): lax.all_to_all(cross_spectrum_product, 'chan', split_axis=3, concat_axis=...  44.6 us
    all_gather x1, blocking collectives, feed_cycles_by_axis(): return jnp.sum(jax.lax.all_gather(inp, chip_axis), axis=0)  31.9 us
    all_to_all x3, local copies, waits for them, and re-layouts, local(): lax.all_to_all(cross_spectrum_product, 'chan', split_axis=3, concat_axis=...  31.4 us
    unnamed x4, local copies, waits for them, and re-layouts  27.5 us
    reshape x1, local copies, waits for them, and re-layouts, stack_segment_windows(): return cross_spectrum_product.reshape(bins, 2, SRC, width)  20.3 us
    dot_general x1, matrix products, local(): lax.dot_general(lax.all_to_all(cross_spectrum_product, 'chan', split_axis...  8.92 us
    another operation x1, other arithmetic  8.65 us
    all_to_all x1, starting transfers between devices, local(): lax.all_to_all(cross_spectrum_product, 'chan', split_axis=3, concat_axis=...  7.63 us
  transfers between devices with their start and end apart: 1, of which 1 were waited for; matrix products, arithmetic and copies ran while one was open for 5% of the time, Pallas kernels for 0%

profile of v1, /device:TPU:32, one launch (start us, length us, event | category | flops | bytes accessed | tf_op | source)
XLA Modules:
  0.0 191.2 jit_solution(4933125321703029951)
XLA Ops:
  0.0 0.0 copy-start
  0.7 1.1 dynamic-slice_select_fusion
  1.8 31.9 %all-gather = bf16[16,30,16,64]{3,2,1,0:T(8,128)(2,1)S(1)} all-gather(bf16[2,30,16,64]{3,2,1,0:T(8,128)(2,1)S(1)} %dynamic-slice_select_fusion), channel_id=2, replica_groups=mesh['chan'=32,'band'=8] {'band'}, dimensions={0}, use_global_device_ids=true | all-gather | bytes 1105920 | tf_op jit(solution)/shard_map/all_gather | solution.py:14
  33.7 0.0 copy-done
  33.7 0.6 fusion.20
  34.3 0.5 reduce_sum.21
  34.8 0.1 copy_multiply_fusion
  35.6 6.7 %divide_convert_fusion = bf16[16,128,1024]{2,1,0:T(8,128)(2,1)} fusion(f32[]{:T(128)S(6)} %convert_element_type.29, bf16[60,16,1024]{2,1,0:T(8,128)(2,1)} %bitcast.32, bf16[30,16,64]{2,0,1:T(8,128)(2,1)S(1)} %fusion.19, bf16[30,16,64]{2,0,1:T(8,128)(2,1)S(1)} %get-tuple-element.6, bf16[30,16,64]{2,0,1:T(8,128)(2,1)S(1)} %get-tuple-element.5), kind=kOutput, calls=%fused_computation | convolution fusion | flops 256835584 | bytes 6344708 | tf_op jit(solution)/shard_map/dot_general | solution.py:41
  42.3 20.3 %copy.14 = bf16[16,2,64,1024]{2,1,0,3:T(2,128)(2,1)} copy(bf16[16,2,64,1024]{3,2,1,0:T(8,128)(2,1)} %bitcast.31) | data formatting | bytes 8388608 | tf_op jit(solution)/shard_map/reshape | solution.py:45
  62.5 13.9 %reshape.166 = bf16[32,2,32768]{2,1,0:T(2,128)(2,1)} reshape(bf16[1024,16,2,64]{3,2,1,0:T(2,128)(2,1)} %bitcast.26) | data formatting | bytes 8388608
  76.4 7.6 %all-to-all-start = ((bf16[32,2,32768]{2,1,0:T(2,128)(2,1)}), bf16[32,2,32768]{2,1,0:T(2,128)(2,1)}, u32[]{:S(2)}, u32[]{:S(2)}) async-start(bf16[32,2,32768]{2,1,0:T(2,128)(2,1)} %reshape.166), calls=%async_computation | async-start | bytes 8388608 | tf_op jit(solution)/shard_map/all_to_all | solution.py:59
  84.1 8.6 %multiply_convert_fusion.1 = (bf16[512,1,1024]{2,0,1:T(8,128)(2,1)S(1)}, bf16[512,1,1024]{2,0,1:T(8,128)(2,1)S(1)}) fusion(s32[1024]{0:T(1024)S(1)} %iota_add_fusion, f32[512]{0:T(512)S(1)} %get-tuple-element.11, f32[512]{0:T(512)S(1)} %get-tuple-element.12), kind=kLoop, calls=%fused_computation.13 | loop fusion | flops 9437184 | bytes 2105344 | tf_op jit(solution)/shard_map/convert.1
  92.7 44.6 %all-to-all-done = bf16[32,2,32768]{2,1,0:T(2,128)(2,1)} async-done(((bf16[32,2,32768]{2,1,0:T(2,128)(2,1)}), bf16[32,2,32768]{2,1,0:T(2,128)(2,1)}, u32[]{:S(2)}, u32[]{:S(2)}) %all-to-all-start) | async-done | bytes 4194336 | tf_op jit(solution)/shard_map/all_to_all | solution.py:59
  137.3 13.6 %reshape.167 = bf16[1024,16,2,64]{3,2,1,0:T(2,128)(2,1)} reshape(bf16[32,2,32768]{2,1,0:T(2,128)(2,1)} %all-to-all-done) | data formatting | bytes 8388608
  151.0 9.8 %copy.15 = bf16[16,2,64,1024]{2,3,1,0:T(8,128)(2,1)} copy(bf16[16,2,64,1024]{2,1,0,3:T(2,128)(2,1)} %bitcast.27) | data formatting | bytes 8388608 | tf_op jit(solution)/shard_map/all_to_all | solution.py:59
  160.8 9.5 %copy.16 = bf16[32,16,2,64,32]{3,4,2,1,0:T(8,128)(2,1)} copy(bf16[32,16,2,64,32]{3,4,0,2,1:T(8,128)(2,1)} %bitcast.28) | data formatting | bytes 8388608 | tf_op jit(solution)/shard_map/all_to_all | solution.py:59
  170.2 12.1 %copy.17 = bf16[512,2,64,32]{0,3,1,2:T(8,128)(2,1)} copy(bf16[512,2,64,32]{2,3,1,0:T(8,128)(2,1)} %bitcast.29) | data formatting | bytes 8388608 | tf_op jit(solution)/shard_map/all_to_all | solution.py:59
  182.3 8.9 %convolution_bitcast_fusion = f32[64,1,32,1024]{3,2,1,0:T(8,128)} fusion(bf16[512,2,64,32]{0,3,1,2:T(8,128)(2,1)} %copy.17, bf16[512,1,1024]{2,0,1:T(8,128)(2,1)S(1)} %get-tuple-element.8, bf16[512,1,1024]{2,0,1:T(8,128)(2,1)S(1)} %get-tuple-element.7), kind=kOutput, calls=%fused_computation.1 | convolution fusion | flops 4296015872 | bytes 14680064 | tf_op jit(solution)/shard_map/dot_general | solution.py:58
  (4 shorter events, 0.0 us)
Async XLA Ops:
  0.0 33.7 %copy-start = (s32[30]{0:T(128)S(1)}, s32[30]{0:T(128)}, u32[]{:S(2)}) copy-start(s32[30]{0:T(128)} %param.5) | copy-start | bytes 364
  76.4 60.9 %all-to-all-start = ((bf16[32,2,32768]{2,1,0:T(2,128)(2,1)}), bf16[32,2,32768]{2,1,0:T(2,128)(2,1)}, u32[]{:S(2)}, u32[]{:S(2)}) async-start(bf16[32,2,32768]{2,1,0:T(2,128)(2,1)} %reshape.166), calls=%async_computation | async-start | bytes 8388608 | tf_op jit(solution)/shard_map/all_to_all | solution.py:59
